TPU v7x, 256 devices: a whole 4x4x8 slice. The times are simulated.
256 devices in a mesh: seq: 64 (over z, y_lo, x), head: 4 (over y_hi, core).
Axes of the slice: x: 4, y: 4 (y_hi: 2, y_lo: 2; y = y_hi * 2 + y_lo), z: 8, core: 2. Of those that a mesh axis runs over, the one named last changes fastest.
Arguments:
- tokens: bfloat16 [32768, 1152], P('seq', 'head'), may hold values from -6 to 6
- cotangent: bfloat16 [32768, 1152], P('seq', 'head'), may hold values from -6 to 6
- qkv_weight: bfloat16 [2, 1152, 3, 1152], P(None, None, None, 'head'), may hold values from -0.14583333 to 0.14583333
- out_weight: bfloat16 [2, 1152, 1152], P(None, 'head'), may hold values from -0.1875 to 0.1875
- modulation: float32 [2, 3, 1152], replicated, may hold values from -3 to 3
- head_gains: float32 [2, 2, 72], replicated, may hold values from 1.2 to 2.2
Outputs:
- mixed: bfloat16 [32768, 1152], P('seq', 'head')
- grad_tokens: bfloat16 [32768, 1152], P('seq', 'head')
All inputs are finite; a program needn't handle non-finite values.
Results may differ from a plain program's by a relative error of at most 0.025.
Values may be sent and summed in bfloat16 or wider, within the bound.
No kernel may reach another device: no remote copies, remote signals or barrier semaphores. Data moves between devices by JAX's collectives and lax.ppermute only.
A program may use at most 128 MiB of HBM per device.

v0:
```python
import jax
import jax.numpy as jnp
from jax import lax
from jax.sharding import PartitionSpec as P

P_SIZE = 512
F_DEV = 1


EPS = 1e-06


def head_norm(values, gains):
    inverse = lax.rsqrt(jnp.mean(values * values, axis=-1, keepdims=True) + EPS)
    return ((values * inverse * gains).astype(jnp.bfloat16), inverse)


def head_back(incoming, normed, inverse, gains):
    grad_f = incoming.astype(jnp.float32)
    norm_f = normed.astype(jnp.float32)
    inner = jnp.mean(norm_f * grad_f, axis=-1, keepdims=True)
    return (inverse * (gains * grad_f - norm_f / gains * inner)).astype(jnp.bfloat16)


def attend(queries, keys, values):
    scaling = queries.shape[-1] ** (-0.5)
    scores = (
        jnp.einsum("glhc,gmhc->ghlm", queries, keys, preferred_element_type=jnp.float32) * scaling
    )
    unnormed = jnp.exp(scores)
    weights = (unnormed / jnp.sum(unnormed, axis=-1, keepdims=True)).astype(jnp.bfloat16)
    return jnp.einsum(
        "ghlm,gmhc->glhc", weights, values, preferred_element_type=jnp.float32
    ).astype(jnp.bfloat16)


def attend_back(queries, keys, values, incoming):
    scaling = queries.shape[-1] ** (-0.5)
    scores = (
        jnp.einsum("glhc,gmhc->ghlm", queries, keys, preferred_element_type=jnp.float32) * scaling
    )
    unnormed = jnp.exp(scores)
    probs = unnormed / jnp.sum(unnormed, axis=-1, keepdims=True)
    weights = probs.astype(jnp.bfloat16)
    grad_probs = jnp.einsum("glhc,gmhc->ghlm", incoming, values, preferred_element_type=jnp.float32)
    grad_values = jnp.einsum(
        "ghlm,glhc->gmhc", weights, incoming, preferred_element_type=jnp.float32
    ).astype(jnp.bfloat16)
    grad_scores = (
        probs * (grad_probs - jnp.sum(grad_probs * probs, axis=-1, keepdims=True))
    ).astype(jnp.bfloat16)
    grad_queries = (
        scaling
        * jnp.einsum("ghlm,gmhc->glhc", grad_scores, keys, preferred_element_type=jnp.float32)
    ).astype(jnp.bfloat16)
    grad_keys = (
        scaling
        * jnp.einsum("ghlm,glhc->gmhc", grad_scores, queries, preferred_element_type=jnp.float32)
    ).astype(jnp.bfloat16)
    return (grad_queries, grad_keys, grad_values)


def across(values):
    return jnp.swapaxes(values, 0, 1)


def prepare(stream, weights_in, modulation, gains):
    full_rows = lax.all_gather(stream, "head", axis=1, tiled=True)
    stream_f = full_rows.astype(jnp.float32)
    row_mean = jnp.mean(stream_f, axis=-1, keepdims=True)
    centred = stream_f - row_mean
    inverse = lax.rsqrt(jnp.mean(centred * centred, axis=-1, keepdims=True) + EPS)
    normed = (centred * inverse * (1.0 + modulation[1]) + modulation[0]).astype(jnp.bfloat16)
    local_width = weights_in.shape[2]
    head_size = gains.shape[-1]
    projected = jnp.dot(
        normed,
        weights_in.reshape(weights_in.shape[0], 3 * local_width),
        preferred_element_type=jnp.float32,
    )
    projected = projected.reshape(stream.shape[0], 3, local_width // head_size, head_size)
    queries, query_inv = head_norm(projected[:, 0], gains[0])
    keys, key_inv = head_norm(projected[:, 1], gains[1])
    values = projected[:, 2].astype(jnp.bfloat16)
    return (row_mean, inverse, queries, keys, values, query_inv, key_inv)


def finish(stream, attended, weights_out, gate_part):
    terms = jnp.dot(
        attended.reshape(stream.shape[0], -1), weights_out, preferred_element_type=jnp.float32
    )
    branch = lax.psum_scatter(
        terms.astype(jnp.bfloat16), "head", scatter_dimension=1, tiled=True
    ).astype(jnp.float32)
    return (stream.astype(jnp.float32) + gate_part * branch).astype(jnp.bfloat16)


def back_start(incoming, weights_out, gate_part, head_size):
    grad_branch = (gate_part * incoming.astype(jnp.float32)).astype(jnp.bfloat16)
    gathered = lax.all_gather(grad_branch, "head", axis=1, tiled=True)
    grad_att = lax.dot_general(
        gathered, weights_out, (((1,), (1,)), ((), ())), preferred_element_type=jnp.float32
    )
    return grad_att.astype(jnp.bfloat16).reshape(incoming.shape[0], -1, head_size)


def back_finish(
    incoming, stream, row_mean, inverse, query_grad, key_grad, value_grad, weights_in, scale_part
):
    count = stream.shape[0]
    stacked = jnp.concatenate(
        [query_grad.reshape(count, -1), key_grad.reshape(count, -1), value_grad.reshape(count, -1)],
        axis=1,
    )
    terms = lax.dot_general(
        stacked,
        weights_in.reshape(weights_in.shape[0], -1),
        (((1,), (1,)), ((), ())),
        preferred_element_type=jnp.float32,
    )
    grad_normed = lax.psum_scatter(
        terms.astype(jnp.bfloat16), "head", scatter_dimension=1, tiled=True
    ).astype(jnp.float32)
    scaled = grad_normed * (1.0 + scale_part)
    centred = (stream.astype(jnp.float32) - row_mean) * inverse
    full_width = stream.shape[1] * lax.axis_size("head")
    sum_first, sum_second = lax.psum(
        (jnp.sum(scaled, axis=1), jnp.sum(scaled * centred, axis=1)), "head"
    )
    first = (sum_first / full_width)[:, None]
    second = (sum_second / full_width)[:, None]
    return (incoming.astype(jnp.float32) + inverse * (scaled - first - centred * second)).astype(
        jnp.bfloat16
    )


def on_device(tokens, cotangent, qkv_weight, out_weight, modulation, head_gains):
    rows, shard = tokens.shape
    head_size = head_gains.shape[-1]
    offset = lax.axis_index("head") * shard

    def slice_of(layer, member):
        return lax.dynamic_slice_in_dim(modulation[layer, member], offset, shard)

    spatial_shape = (F_DEV, P_SIZE, -1, head_size)
    stored_s = prepare(tokens, qkv_weight[0], modulation[0], head_gains[0])
    attended_s = attend(
        stored_s[2].reshape(spatial_shape),
        stored_s[3].reshape(spatial_shape),
        stored_s[4].reshape(spatial_shape),
    )
    middle = finish(tokens, attended_s, out_weight[0], slice_of(0, 2))
    stored_t = prepare(middle, qkv_weight[1], modulation[1], head_gains[1])
    queries = lax.all_to_all(
        stored_t[2].reshape(spatial_shape), "seq", split_axis=1, concat_axis=0, tiled=True
    )
    keys = lax.all_to_all(
        stored_t[3].reshape(spatial_shape), "seq", split_axis=1, concat_axis=0, tiled=True
    )
    values = lax.all_to_all(
        stored_t[4].reshape(spatial_shape), "seq", split_axis=1, concat_axis=0, tiled=True
    )
    attended_t = across(attend(across(queries), across(keys), across(values)))
    returned = lax.all_to_all(attended_t, "seq", split_axis=0, concat_axis=1, tiled=True)
    mixed = finish(middle, returned, out_weight[1], slice_of(1, 2))
    grad_att = back_start(cotangent, out_weight[1], slice_of(1, 2), head_size)
    moved_grad = lax.all_to_all(
        grad_att.reshape(spatial_shape), "seq", split_axis=1, concat_axis=0, tiled=True
    )
    grad_q, grad_k, grad_v = attend_back(
        across(queries), across(keys), across(values), across(moved_grad)
    )
    back_q, back_k, back_v = (
        lax.all_to_all(across(grad_q), "seq", split_axis=0, concat_axis=1, tiled=True),
        lax.all_to_all(across(grad_k), "seq", split_axis=0, concat_axis=1, tiled=True),
        lax.all_to_all(across(grad_v), "seq", split_axis=0, concat_axis=1, tiled=True),
    )
    query_grad = head_back(
        back_q.reshape(rows, -1, head_size), stored_t[2], stored_t[5], head_gains[1, 0]
    )
    key_grad = head_back(
        back_k.reshape(rows, -1, head_size), stored_t[3], stored_t[6], head_gains[1, 1]
    )
    grad_middle = back_finish(
        cotangent,
        middle,
        stored_t[0],
        stored_t[1],
        query_grad,
        key_grad,
        back_v,
        qkv_weight[1],
        slice_of(1, 1),
    )
    grad_att_s = back_start(grad_middle, out_weight[0], slice_of(0, 2), head_size)
    grad_q_s, grad_k_s, grad_v_s = attend_back(
        stored_s[2].reshape(spatial_shape),
        stored_s[3].reshape(spatial_shape),
        stored_s[4].reshape(spatial_shape),
        grad_att_s.reshape(spatial_shape),
    )
    query_grad_s = head_back(
        grad_q_s.reshape(rows, -1, head_size), stored_s[2], stored_s[5], head_gains[0, 0]
    )
    key_grad_s = head_back(
        grad_k_s.reshape(rows, -1, head_size), stored_s[3], stored_s[6], head_gains[0, 1]
    )
    grad_tokens = back_finish(
        grad_middle,
        tokens,
        stored_s[0],
        stored_s[1],
        query_grad_s,
        key_grad_s,
        grad_v_s,
        qkv_weight[0],
        slice_of(0, 1),
    )
    return (mixed, grad_tokens)


def solution(mesh):
    in_specs = (
        P("seq", "head"),
        P("seq", "head"),
        P(None, None, None, "head"),
        P(None, "head", None),
        P(),
        P(),
    )
    out_specs = (P("seq", "head"), P("seq", "head"))
    return jax.shard_map(
        on_device, mesh=mesh, in_specs=in_specs, out_specs=out_specs, check_vma=False
    )
```

profile of v0, /device:TPU:1, one launch (start us, length us, event | category | flops | bytes accessed | tf_op | source)
XLA Modules:
  0.0 483.5 jit_solution(92628475510384482)
XLA Ops:
  10.6 4.3 fusion.148
  15.0 23.1 %all-gather.5.cloned.1.call-done = bf16[512,1152]{0,1:T(8,128)(2,1)} async-done(((bf16[512,288]{0,1:T(8,128)(2,1)}), bf16[512,1152]{0,1:T(8,128)(2,1)}) %all-gather.5.cloned.1.call-update) | async-done | bytes 1179664 | tf_op jit(solution)/shard_map/all_gather | solution.py:68
  41.4 3.0 fusion.24
  48.4 1.9 convolution_convert_fusion.3
  52.1 35.2 %reduce-scatter.5.cloned.1.call-done = bf16[512,288]{0,1:T(8,128)(2,1)} async-done(((bf16[512,1152]{0,1:T(8,128)(2,1)}), bf16[512,288]{0,1:T(8,128)(2,1)}) %reduce-scatter.5.cloned.1.call-update) | async-done | bytes 294928 | tf_op jit(solution)/shard_map/reduce_scatter | solution.py:92
  89.2 24.6 %all-gather.9.cloned.1.call-done = bf16[512,1152]{0,1:T(8,128)(2,1)} async-done(((bf16[512,288]{0,1:T(8,128)(2,1)}), bf16[512,1152]{0,1:T(8,128)(2,1)}) %all-gather.9.cloned.1.call-update) | async-done | bytes 1179664 | tf_op jit(solution)/shard_map/all_gather | solution.py:100
  113.8 2.0 convolution_convert_fusion.7
  116.9 10.4 %all-to-all-start.4 = ((bf16[1,512,4,72]{3,2,0,1:T(4,128)(2,1)}), bf16[1,512,4,72]{3,2,0,1:T(4,128)(2,1)}, u32[]{:S(2)}, u32[]{:S(2)}) async-start(bf16[1,512,4,72]{3,2,0,1:T(4,128)(2,1)} %copy.135), calls=%async_computation.6 | async-start | bytes 1048576 | tf_op jit(solution)/shard_map/all_to_all | solution.py:167
  127.4 17.2 %all-gather.7.cloned.1.call-done = bf16[512,1152]{0,1:T(8,128)(2,1)} async-done(((bf16[512,288]{0,1:T(8,128)(2,1)}), bf16[512,1152]{0,1:T(8,128)(2,1)}) %all-gather.7.cloned.1.call-update) | async-done | bytes 1179664 | tf_op jit(solution)/shard_map/all_gather | solution.py:68
  147.9 3.0 fusion.27
  152.1 2.1 copy.127
  154.1 10.0 %all-to-all-start.1 = ((bf16[1,512,4,72]{3,2,0,1:T(4,128)(2,1)}), bf16[1,512,4,72]{3,2,0,1:T(4,128)(2,1)}, u32[]{:S(2)}, u32[]{:S(2)}) async-start(bf16[1,512,4,72]{3,2,0,1:T(4,128)(2,1)} %copy.127), calls=%async_computation.2 | async-start | bytes 1048576 | tf_op jit(solution)/shard_map/all_to_all | solution.py:154
  164.1 2.1 copy.130
  166.2 14.0 %all-to-all-done.1 = bf16[1,512,4,72]{3,2,0,1:T(4,128)(2,1)} async-done(((bf16[1,512,4,72]{3,2,0,1:T(4,128)(2,1)}), bf16[1,512,4,72]{3,2,0,1:T(4,128)(2,1)}, u32[]{:S(2)}, u32[]{:S(2)}) %all-to-all-start.1) | async-done | bytes 294944 | tf_op jit(solution)/shard_map/all_to_all | solution.py:154
  180.2 7.0 %all-to-all-start.2 = ((bf16[1,512,4,72]{3,2,0,1:T(4,128)(2,1)}), bf16[1,512,4,72]{3,2,0,1:T(4,128)(2,1)}, u32[]{:S(2)}, u32[]{:S(2)}) async-start(bf16[1,512,4,72]{3,2,0,1:T(4,128)(2,1)} %copy.130), calls=%async_computation.3 | async-start | bytes 1048576 | tf_op jit(solution)/shard_map/all_to_all | solution.py:157
  188.0 2.0 copy.124
  190.0 11.8 %all-to-all-done.2 = bf16[1,512,4,72]{3,2,0,1:T(4,128)(2,1)} async-done(((bf16[1,512,4,72]{3,2,0,1:T(4,128)(2,1)}), bf16[1,512,4,72]{3,2,0,1:T(4,128)(2,1)}, u32[]{:S(2)}, u32[]{:S(2)}) %all-to-all-start.2) | async-done | bytes 294944 | tf_op jit(solution)/shard_map/all_to_all | solution.py:157
  201.8 8.0 %all-to-all-start = ((bf16[1,512,4,72]{3,2,0,1:T(4,128)(2,1)}), bf16[1,512,4,72]{3,2,0,1:T(4,128)(2,1)}, u32[]{:S(2)}, u32[]{:S(2)}) async-start(bf16[1,512,4,72]{3,2,0,1:T(4,128)(2,1)} %copy.124), calls=%async_computation.1 | async-start | bytes 1048576 | tf_op jit(solution)/shard_map/all_to_all | solution.py:160
  213.7 10.3 %all-to-all-done = bf16[1,512,4,72]{3,2,0,1:T(4,128)(2,1)} async-done(((bf16[1,512,4,72]{3,2,0,1:T(4,128)(2,1)}), bf16[1,512,4,72]{3,2,0,1:T(4,128)(2,1)}, u32[]{:S(2)}, u32[]{:S(2)}) %all-to-all-start) | async-done | bytes 294944 | tf_op jit(solution)/shard_map/all_to_all | solution.py:160
  224.0 2.2 multiply_reduce_fusion.1
  229.9 8.4 %all-to-all-start.5 = ((bf16[64,8,4,72]{3,2,1,0:T(4,128)(2,1)}), bf16[64,8,4,72]{3,2,1,0:T(4,128)(2,1)}, u32[]{:S(2)}, u32[]{:S(2)}) async-start(bf16[64,8,4,72]{3,2,1,0:T(4,128)(2,1)} %copy.139), calls=%async_computation.7 | async-start | bytes 1048576 | tf_op jit(solution)/shard_map/all_to_all | solution.py:174
  241.1 11.4 %all-to-all-done.5 = bf16[64,8,4,72]{3,2,1,0:T(4,128)(2,1)} async-done(((bf16[64,8,4,72]{3,2,1,0:T(4,128)(2,1)}), bf16[64,8,4,72]{3,2,1,0:T(4,128)(2,1)}, u32[]{:S(2)}, u32[]{:S(2)}) %all-to-all-start.5) | async-done | bytes 294944 | tf_op jit(solution)/shard_map/all_to_all | solution.py:174
  252.5 8.4 %all-to-all-start.6 = ((bf16[64,8,4,72]{3,2,1,0:T(4,128)(2,1)}), bf16[64,8,4,72]{3,2,1,0:T(4,128)(2,1)}, u32[]{:S(2)}, u32[]{:S(2)}) async-start(bf16[64,8,4,72]{3,2,1,0:T(4,128)(2,1)} %copy.143), calls=%async_computation.8 | async-start | bytes 1048576 | tf_op jit(solution)/shard_map/all_to_all | solution.py:175
  267.0 3.1 fusion.20
  270.1 2.2 copy.147
  272.4 2.1 convert_element_type.406
  274.5 2.4 copy.142
  276.9 10.8 %all-to-all-start.7 = ((bf16[64,8,4,72]{3,2,1,0:T(4,128)(2,1)}), bf16[64,8,4,72]{3,2,1,0:T(4,128)(2,1)}, u32[]{:S(2)}, u32[]{:S(2)}) async-start(bf16[64,8,4,72]{3,2,1,0:T(4,128)(2,1)} %copy.147), calls=%async_computation.9 | async-start | bytes 1048576 | tf_op jit(solution)/shard_map/all_to_all | solution.py:176
  288.0 2.1 convert_element_type.408
  290.1 2.4 copy.146
  292.5 2.3 reshape.364
  294.8 2.2 copy.140
  297.0 2.3 reshape.366
  299.3 2.2 copy.144
  307.4 2.5 convolution_convert_fusion.1
  310.0 2.2 fusion.19
  312.7 23.9 %all_to_all.84 = bf16[64,8,4,72]{3,2,1,0:T(4,128)(2,1)S(1)} all-to-all(bf16[64,8,4,72]{3,2,1,0:T(4,128)(2,1)S(1)} %copy.134), channel_id=1, replica_groups=mesh['seq'=64,'head'=4] {'seq'}, dimensions={0} | all-to-all | bytes 589824 | tf_op jit(solution)/shard_map/all_to_all | solution.py:164
  337.0 3.0 convolution_convert_fusion.2
  340.9 9.3 %reduce-scatter.9.cloned.1.call-done = bf16[512,288]{0,1:T(8,128)(2,1)} async-done(((bf16[512,1152]{0,1:T(8,128)(2,1)}), bf16[512,288]{0,1:T(8,128)(2,1)}) %reduce-scatter.9.cloned.1.call-update) | async-done | bytes 294928 | tf_op jit(solution)/shard_map/reduce_scatter | solution.py:121
  351.3 7.2 %all-reduce.1 = (f32[512]{0:T(512)S(1)}, f32[512]{0:T(512)S(1)}) all-reduce(f32[512]{0:T(512)S(1)} %get-tuple-element.11, f32[512]{0:T(512)S(1)} %get-tuple-element.10), channel_id=1, replica_groups=mesh['seq'=64,'head'=4] {'head'}, use_global_device_ids=true, to_apply=%region_19.0 | all-reduce | flops 1024 | bytes 8192 | tf_op jit(solution)/shard_map/psum | solution.py:127
  358.5 31.5 %reduce-scatter.7.cloned.1.call-done = bf16[512,288]{0,1:T(8,128)(2,1)} async-done(((bf16[512,1152]{0,1:T(8,128)(2,1)}), bf16[512,288]{0,1:T(8,128)(2,1)}) %reduce-scatter.7.cloned.1.call-update) | async-done | bytes 294928 | tf_op jit(solution)/shard_map/reduce_scatter | solution.py:92
  390.0 2.2 fusion.73
  392.9 23.6 %all-gather.11.cloned.1.call-done = bf16[512,1152]{0,1:T(8,128)(2,1)} async-done(((bf16[512,288]{0,1:T(8,128)(2,1)}), bf16[512,1152]{0,1:T(8,128)(2,1)}) %all-gather.11.cloned.1.call-update) | async-done | bytes 1179664 | tf_op jit(solution)/shard_map/all_gather | solution.py:100
  416.5 2.0 convolution_convert_fusion.6
  418.5 3.4 multiply_reduce_fusion
  426.9 2.4 convolution_convert_fusion
  430.1 36.2 %reduce-scatter.11.cloned.1.call-done = bf16[512,288]{0,1:T(8,128)(2,1)} async-done(((bf16[512,1152]{0,1:T(8,128)(2,1)}), bf16[512,288]{0,1:T(8,128)(2,1)}) %reduce-scatter.11.cloned.1.call-update) | async-done | bytes 294928 | tf_op jit(solution)/shard_map/reduce_scatter | solution.py:121
  467.5 7.2 %all-reduce = (f32[512]{0:T(512)S(1)}, f32[512]{0:T(512)S(1)}) all-reduce(f32[512]{0:T(512)S(1)} %get-tuple-element.9, f32[512]{0:T(512)S(1)} %get-tuple-element.8), channel_id=1, replica_groups=mesh['seq'=64,'head'=4] {'head'}, use_global_device_ids=true, to_apply=%region_27.0 | all-reduce | flops 1024 | bytes 8192 | tf_op jit(solution)/shard_map/psum | solution.py:127
  (181 shorter events, 55.1 us)
Async XLA Ops:
  7.2 31.0 %all-gather.5.cloned.1.call-start = ((), (), s32[]{:S(2)}) async-start(), calls=%async_computation.12 | async-start | bytes 1474560 | tf_op jit(solution)/shard_map/all_gather | solution.py:68
  7.9 79.5 %reduce-scatter.5.cloned.1.call-start = ((), (), s32[]{:S(2)}) async-start(), calls=%async_computation.13 | async-start | bytes 1474560 | tf_op jit(solution)/shard_map/reduce_scatter | solution.py:92
  9.2 35.4 %copy-start.43 = (f32[72]{0:T(128)}, f32[72]{0:T(128)S(1)}, u32[]{:S(2)}) copy-start(f32[72]{0:T(128)S(1)} %get-tuple-element.38) | copy-start | bytes 868
  9.2 35.4 %copy-start.45 = (f32[72]{0:T(128)}, f32[72]{0:T(128)S(1)}, u32[]{:S(2)}) copy-start(f32[72]{0:T(128)S(1)} %get-tuple-element.39) | copy-start | bytes 868
  38.1 3.3 copy-start.8
  39.7 4.7 copy-start.28
  41.4 3.0 copy-start.32
  46.1 1.9 copy-start
  46.1 1.9 copy-start.26
  46.1 2.3 copy-start.20
  48.0 3.1 copy-start.17
  48.4 38.9 %copy-start.10 = (bf16[512,288]{0,1:T(8,128)(2,1)S(1)}, bf16[512,288]{0,1:T(8,128)(2,1)}, u32[]{:S(2)}) copy-start(bf16[512,288]{0,1:T(8,128)(2,1)} %param.6) | copy-start | bytes 884740
  50.4 63.5 %all-gather.9.cloned.1.call-start = ((), (), s32[]{:S(2)}) async-start(), calls=%async_computation.16 | async-start | bytes 1474560 | tf_op jit(solution)/shard_map/all_gather | solution.py:100
  52.0 92.6 %all-gather.7.cloned.1.call-start = ((), (), s32[]{:S(2)}) async-start(), calls=%async_computation.14 | async-start | bytes 1474560 | tf_op jit(solution)/shard_map/all_gather | solution.py:68
  52.1 64.8 %copy-start.36 = (f32[288]{0:T(512)}, f32[288]{0:T(512)S(1)}, u32[]{:S(2)}) copy-start(f32[288]{0:T(512)S(1)} %dynamic-slice_reduce_fusion.1) | copy-start | bytes 3460
  116.9 37.2 %all-to-all-start.4 = ((bf16[1,512,4,72]{3,2,0,1:T(4,128)(2,1)}), bf16[1,512,4,72]{3,2,0,1:T(4,128)(2,1)}, u32[]{:S(2)}, u32[]{:S(2)}) async-start(bf16[1,512,4,72]{3,2,0,1:T(4,128)(2,1)} %copy.135), calls=%async_computation.6 | async-start | bytes 1048576 | tf_op jit(solution)/shard_map/all_to_all | solution.py:167
  144.6 3.3 copy-start.9
  146.2 4.7 copy-start.30
  147.8 3.0 copy-start.38
  147.8 3.2 copy-start.41
  147.9 3.2 copy-start.42
  154.1 26.1 %all-to-all-start.1 = ((bf16[1,512,4,72]{3,2,0,1:T(4,128)(2,1)}), bf16[1,512,4,72]{3,2,0,1:T(4,128)(2,1)}, u32[]{:S(2)}, u32[]{:S(2)}) async-start(bf16[1,512,4,72]{3,2,0,1:T(4,128)(2,1)} %copy.127), calls=%async_computation.2 | async-start | bytes 1048576 | tf_op jit(solution)/shard_map/all_to_all | solution.py:154
  180.2 21.6 %all-to-all-start.2 = ((bf16[1,512,4,72]{3,2,0,1:T(4,128)(2,1)}), bf16[1,512,4,72]{3,2,0,1:T(4,128)(2,1)}, u32[]{:S(2)}, u32[]{:S(2)}) async-start(bf16[1,512,4,72]{3,2,0,1:T(4,128)(2,1)} %copy.130), calls=%async_computation.3 | async-start | bytes 1048576 | tf_op jit(solution)/shard_map/all_to_all | solution.py:157
  201.8 22.2 %all-to-all-start = ((bf16[1,512,4,72]{3,2,0,1:T(4,128)(2,1)}), bf16[1,512,4,72]{3,2,0,1:T(4,128)(2,1)}, u32[]{:S(2)}, u32[]{:S(2)}) async-start(bf16[1,512,4,72]{3,2,0,1:T(4,128)(2,1)} %copy.124), calls=%async_computation.1 | async-start | bytes 1048576 | tf_op jit(solution)/shard_map/all_to_all | solution.py:160
  224.0 2.2 copy-start.12
  229.9 22.6 %all-to-all-start.5 = ((bf16[64,8,4,72]{3,2,1,0:T(4,128)(2,1)}), bf16[64,8,4,72]{3,2,1,0:T(4,128)(2,1)}, u32[]{:S(2)}, u32[]{:S(2)}) async-start(bf16[64,8,4,72]{3,2,1,0:T(4,128)(2,1)} %copy.139), calls=%async_computation.7 | async-start | bytes 1048576 | tf_op jit(solution)/shard_map/all_to_all | solution.py:174
  252.5 24.4 %all-to-all-start.6 = ((bf16[64,8,4,72]{3,2,1,0:T(4,128)(2,1)}), bf16[64,8,4,72]{3,2,1,0:T(4,128)(2,1)}, u32[]{:S(2)}, u32[]{:S(2)}) async-start(bf16[64,8,4,72]{3,2,1,0:T(4,128)(2,1)} %copy.143), calls=%async_computation.8 | async-start | bytes 1048576 | tf_op jit(solution)/shard_map/all_to_all | solution.py:175
  276.9 26.2 %all-to-all-start.7 = ((bf16[64,8,4,72]{3,2,1,0:T(4,128)(2,1)}), bf16[64,8,4,72]{3,2,1,0:T(4,128)(2,1)}, u32[]{:S(2)}, u32[]{:S(2)}) async-start(bf16[64,8,4,72]{3,2,1,0:T(4,128)(2,1)} %copy.147), calls=%async_computation.9 | async-start | bytes 1048576 | tf_op jit(solution)/shard_map/all_to_all | solution.py:176
  287.7 62.4 %reduce-scatter.9.cloned.1.call-start = ((), (), s32[]{:S(2)}) async-start(), calls=%async_computation.17 | async-start | bytes 1474560 | tf_op jit(solution)/shard_map/reduce_scatter | solution.py:121
  303.0 4.1 copy-start.13
  303.0 4.1 copy-start.14
  303.0 4.1 copy-start.40
  309.9 80.1 %reduce-scatter.7.cloned.1.call-start = ((), (), s32[]{:S(2)}) async-start(), calls=%async_computation.15 | async-start | bytes 1474560 | tf_op jit(solution)/shard_map/reduce_scatter | solution.py:92
  336.6 13.5 %copy-start.7 = (bf16[512,288]{0,1:T(8,128)(2,1)S(1)}, bf16[512,288]{0,1:T(8,128)(2,1)}, u32[]{:S(2)}) copy-start(bf16[512,288]{0,1:T(8,128)(2,1)} %fusion.57) | copy-start | bytes 884740
  336.6 13.5 %copy-start.31 = (f32[512]{0:T(512)S(1)}, f32[512]{0:T(512)}, u32[]{:S(2)}) copy-start(f32[512]{0:T(512)} %copy-done.30) | copy-start | bytes 6148
  336.6 13.5 %copy-start.39 = (f32[512]{0:T(512)S(1)}, f32[512]{0:T(512)}, u32[]{:S(2)}) copy-start(f32[512]{0:T(512)} %copy-done.38) | copy-start | bytes 6148
  337.0 53.1 %copy-start.18 = (bf16[512,288]{0,1:T(8,128)(2,1)S(1)}, bf16[512,288]{0,1:T(8,128)(2,1)}, u32[]{:S(2)}) copy-start(bf16[512,288]{0,1:T(8,128)(2,1)} %param.7) | copy-start | bytes 884740
  337.0 53.1 %copy-start.35 = (f32[288]{0:T(512)S(1)}, f32[288]{0:T(512)}, u32[]{:S(2)}) copy-start(f32[288]{0:T(512)} %copy-done.34) | copy-start | bytes 3460
  337.0 53.1 %copy-start.37 = (f32[288]{0:T(512)S(1)}, f32[288]{0:T(512)}, u32[]{:S(2)}) copy-start(f32[288]{0:T(512)} %copy-done.36) | copy-start | bytes 3460
  340.0 52.6 %copy-start.46 = (f32[72]{0:T(128)S(1)}, f32[72]{0:T(128)}, u32[]{:S(2)}) copy-start(f32[72]{0:T(128)} %copy-done.45) | copy-start | bytes 868
  340.0 52.7 %copy-start.44 = (f32[72]{0:T(128)S(1)}, f32[72]{0:T(128)}, u32[]{:S(2)}) copy-start(f32[72]{0:T(128)} %copy-done.43) | copy-start | bytes 868
  340.0 76.5 %all-gather.11.cloned.1.call-start = ((), (), s32[]{:S(2)}) async-start(), calls=%async_computation.18 | async-start | bytes 1474560 | tf_op jit(solution)/shard_map/all_gather | solution.py:100
  392.3 74.1 %reduce-scatter.11.cloned.1.call-start = ((), (), s32[]{:S(2)}) async-start(), calls=%async_computation.19 | async-start | bytes 1474560 | tf_op jit(solution)/shard_map/reduce_scatter | solution.py:121
  392.8 25.7 %copy-start.27 = (f32[4,512]{1,0:T(4,128)S(1)}, f32[4,512]{1,0:T(4,128)}, u32[]{:S(2)}) copy-start(f32[4,512]{1,0:T(4,128)} %copy-done.26) | copy-start | bytes 24580
  418.5 3.5 copy-start.1
  426.9 39.5 %copy-start.11 = (bf16[512,288]{0,1:T(8,128)(2,1)S(1)}, bf16[512,288]{0,1:T(8,128)(2,1)}, u32[]{:S(2)}) copy-start(bf16[512,288]{0,1:T(8,128)(2,1)} %param.6) | copy-start | bytes 884740
  426.9 39.5 %copy-start.29 = (f32[512]{0:T(512)S(1)}, f32[512]{0:T(512)}, u32[]{:S(2)}) copy-start(f32[512]{0:T(512)} %copy-done.28) | copy-start | bytes 6148
  426.9 39.5 %copy-start.33 = (f32[512]{0:T(512)S(1)}, f32[512]{0:T(512)}, u32[]{:S(2)}) copy-start(f32[512]{0:T(512)} %copy-done.32) | copy-start | bytes 6148
  (14 other events, 16.0 us)
Sparse Core Ops, SparseCore 0:
  9.8 28.2 all-gather.4
  50.5 36.8 reduce-scatter.4
  89.9 23.8 all-gather.8
  116.2 28.3 all-gather.6
  310.1 40.0 reduce-scatter.8
  352.8 37.1 reduce-scatter.6
  392.5 23.8 all-gather.10
  429.5 36.8 reduce-scatter.10
where the time goes:
time: 486 us; the launch traced here: 484 us
  waiting for transfers between devices  249 us (51%)
  starting transfers between devices  63.9 us (13%)
  local copies, waits for them, and re-layouts  47.4 us (10%)
  matrix products  39.2 us (8%)
  blocking collectives  38.4 us (8%)
  other arithmetic  30.6 us (6%)
  between operations  14.9 us (3%)
    reduce_scatter x2, waiting for transfers between devices, finish(): lax.psum_scatter(terms.astype(jnp.bfloat16), 'head', scatter_dimension=1,...  66.8 us
    all_gather x2, waiting for transfers between devices, back_start(): gathered = lax.all_gather(grad_branch, 'head', axis=1, tiled=True)  48.2 us
    reduce_scatter x2, waiting for transfers between devices, back_finish(): lax.psum_scatter(terms.astype(jnp.bfloat16), 'head', scatter_dimension=1,...  45.5 us
    all_gather x2, waiting for transfers between devices, prepare(): full_rows = lax.all_gather(stream, 'head', axis=1, tiled=True)  40.3 us
    all_to_all x1, blocking collectives, on_device(): lax.all_to_all(attended_t, 'seq', split_axis=0, concat_axis=1, tiled=True)  23.9 us
    psum x2, blocking collectives, back_finish(): lax.psum((jnp.sum(scaled, axis=1), jnp.sum(scaled * centred, axis=1)), 'h...  14.4 us
    all_to_all x1, waiting for transfers between devices, on_device(): lax.all_to_all(stored_t[2].reshape(spatial_shape), 'seq', split_axis=1, c...  14 us
    convert_element_type x6, local copies, waits for them, and re-layouts, head_back(): grad_f = incoming.astype(jnp.float32)  13.7 us
  transfers between devices with their start and end apart: 15, of which 12 were waited for; matrix products, arithmetic and copies ran while one was open for 15% of the time, Pallas kernels for 0%

commit v1 on v0

v1 whole, which is shorter than its diff:
```python
import jax
import jax.numpy as jnp
from jax import lax
from jax.experimental import pallas as pl
from jax.experimental.pallas import tpu as pltpu
from jax.sharding import PartitionSpec as P

EPS = 1e-06
HEAD = 72
PER = 4
WIDE = 1152
PART = 288
ROWS = 512
OWN = 128
LOG2E = 1.4426950408889634
SCALE = HEAD**-0.5
F32 = jnp.float32
BF16 = jnp.bfloat16
VMEM_LIMIT = 56 * 1024 * 1024


def dot(a, b, over):
    return lax.dot_general(a, b, (((over[0],), (over[1],)), ((), ())), preferred_element_type=F32)


def call(body, outs, operands, scratch=(), flops=0, smem=0):
    size = sum(o.size * o.dtype.itemsize for o in (*outs, *operands))
    specs = [
        pl.BlockSpec(memory_space=pltpu.SMEM) if i < smem else pl.BlockSpec(memory_space=pltpu.VMEM)
        for i in range(len(operands))
    ]
    return pl.pallas_call(
        body,
        out_shape=list(outs),
        in_specs=specs,
        out_specs=[pl.BlockSpec(memory_space=pltpu.VMEM)] * len(outs),
        scratch_shapes=list(scratch),
        compiler_params=pltpu.CompilerParams(vmem_limit_bytes=VMEM_LIMIT),
        cost_estimate=pl.CostEstimate(flops=flops, bytes_accessed=size, transcendentals=0),
    )(*operands)


def out(shape, dtype=BF16):
    return jax.ShapeDtypeStruct(shape, dtype)


def head_norm_t(part, gains):
    n = part.shape[1]
    cube = part.reshape(PER, HEAD, n)
    inverse = lax.rsqrt(jnp.sum(cube * cube, axis=1, keepdims=True) * (1.0 / HEAD) + EPS)
    return (cube * inverse * gains.reshape(PER, HEAD, 1)).reshape(PART, n).astype(BF16), inverse


def head_back_t(incoming, normed, inverse, gains):
    n = incoming.shape[1]
    grad = incoming.astype(F32).reshape(PER, HEAD, n)
    norm = normed.astype(F32).reshape(PER, HEAD, n)
    gain = gains.reshape(PER, HEAD, 1)
    inner = jnp.sum(norm * grad, axis=1, keepdims=True) * (1.0 / HEAD)
    return (inverse * (gain * grad - norm * (1.0 / gain) * inner)).reshape(PART, n).astype(BF16)


def spatial_forward(
    me_ref, x0, x1, x2, x3, modc, gains, wt, wo, q_o, k_o, v_o, st_o, p0, p1, p2, p3, xrow, xs
):
    me = me_ref[0]
    for d, x in enumerate((x0, x1, x2, x3)):
        xs[pl.ds(pl.multiple_of((me ^ d) * PART, 32), PART), :] = x[...]
    stream = xs[...].astype(F32)
    mean = jnp.sum(stream, axis=0, keepdims=True) * (1.0 / WIDE)
    centred = stream - mean
    inverse = lax.rsqrt(jnp.sum(centred * centred, axis=0, keepdims=True) * (1.0 / WIDE) + EPS)
    normed = (centred * inverse * (1.0 + modc[:, 1:2]) + modc[:, 0:1]).astype(BF16)
    projected = dot(wt[...].reshape(3 * PART, WIDE), normed, (1, 0))
    query, inv_q = head_norm_t(projected[:PART], gains[:, 0:1])
    key, inv_k = head_norm_t(projected[PART : 2 * PART], gains[:, 1:2])
    q_o[...] = query
    k_o[...] = key
    v_o[...] = projected[2 * PART :].astype(BF16)
    st_o[0:4, :] = inv_q.reshape(PER, ROWS)
    st_o[4:8, :] = inv_k.reshape(PER, ROWS)
    st_o[8:9, :] = mean
    st_o[9:10, :] = inverse
    for d, partial in ((3, p3), (2, p2), (1, p1), (0, p0)):
        columns = pl.ds(pl.multiple_of((me ^ d) * OWN, OWN), OWN)
        queries = q_o[:, columns]
        pieces = []
        for h in range(PER):
            rows = slice(h * HEAD, (h + 1) * HEAD)
            scores = dot(k_o[rows, :], queries[rows], (0, 0))
            unnormed = jnp.exp2(scores * (SCALE * LOG2E))
            total = jnp.sum(unnormed, axis=0, keepdims=True)
            pieces.append(dot(v_o[rows, :], unnormed.astype(BF16), (1, 0)) * (1.0 / total))
        attended = jnp.concatenate(pieces, axis=0).astype(BF16)
        partial[...] = dot(attended, wo[...], (0, 0)).astype(BF16)
    own = xs[:, pl.ds(pl.multiple_of(me * OWN, OWN), OWN)].astype(F32)
    xrow[...] = own.T.astype(BF16)


def temporal(
    x0, x1, c0, c1, modr, gains, wt_a, wo_a, wt_b, wo_b, gn0, gn1, op0, op1
):
    stream = jnp.concatenate([x0[...], x1[...]], axis=0).astype(F32)
    incoming = jnp.concatenate([c0[...], c1[...]], axis=0).astype(F32)
    mean = jnp.sum(stream, axis=1, keepdims=True) * (1.0 / WIDE)
    centred = stream - mean
    inverse = lax.rsqrt(jnp.sum(centred * centred, axis=1, keepdims=True) * (1.0 / WIDE) + EPS)
    normed = (centred * inverse * (1.0 + modr[1:2, :]) + modr[0:1, :]).astype(BF16)
    gated = (modr[2:3, :] * incoming).astype(BF16)
    n = stream.shape[0]
    left = lax.broadcasted_iota(jnp.int32, (n, n), 0)
    right = lax.broadcasted_iota(jnp.int32, (n, n), 1)
    mask = ((left & 1) == (right & 1)) & ((left // OWN) == (right // OWN))
    branch = None
    grad_normed = None
    for wt, wo in ((wt_a, wo_a), (wt_b, wo_b)):
        weights = wt[...].reshape(3 * PART, WIDE)
        projected = dot(weights, normed, (1, 1))
        query, inv_q = head_norm_t(projected[:PART], gains[:, 0:1])
        key, inv_k = head_norm_t(projected[PART : 2 * PART], gains[:, 1:2])
        value = projected[2 * PART :].astype(BF16)
        grad_att = dot(wo[...], gated, (1, 1)).astype(BF16)
        attended, gq, gk, gv = [], [], [], []
        for h in range(PER):
            rows = slice(h * HEAD, (h + 1) * HEAD)
            q, k, v, da = query[rows], key[rows], value[rows], grad_att[rows]
            scores = dot(k, q, (0, 0))
            unnormed = jnp.where(mask, jnp.exp2(scores * (SCALE * LOG2E)), 0.0)
            probs = unnormed * (1.0 / jnp.sum(unnormed, axis=0, keepdims=True))
            rounded = probs.astype(BF16)
            attended.append(dot(v, rounded, (1, 0)))
            grad_probs = dot(v, da, (0, 0))
            inner = jnp.sum(grad_probs * probs, axis=0, keepdims=True)
            grad_scores = (probs * (grad_probs - inner)).astype(BF16)
            gv.append(dot(da, rounded, (1, 1)))
            gq.append(dot(k, grad_scores, (1, 0)) * SCALE)
            gk.append(dot(q, grad_scores, (1, 1)) * SCALE)
        attended = jnp.concatenate(attended, axis=0).astype(BF16)
        gq = jnp.concatenate(gq, axis=0).astype(BF16)
        gk = jnp.concatenate(gk, axis=0).astype(BF16)
        gv = jnp.concatenate(gv, axis=0).astype(BF16)
        dq = head_back_t(gq, query, inv_q, gains[:, 0:1])
        dk = head_back_t(gk, key, inv_k, gains[:, 1:2])
        stacked = jnp.concatenate([dq, dk, gv], axis=0)
        term = dot(stacked, weights, (0, 0))
        grad_normed = term if grad_normed is None else grad_normed + term
        term = dot(attended, wo[...], (0, 0))
        branch = term if branch is None else branch + term
    gn0[...] = grad_normed[:OWN]
    gn1[...] = grad_normed[OWN:].astype(BF16)
    op0[...] = branch[:OWN]
    op1[...] = branch[OWN:].astype(BF16)


def temporal_finish(x0, c0, gn0, gn1, op0, op1, modr, gm_o, mixed_o):
    stream = x0[...].astype(F32)
    mean = jnp.sum(stream, axis=1, keepdims=True) * (1.0 / WIDE)
    shifted = stream - mean
    inverse = lax.rsqrt(jnp.sum(shifted * shifted, axis=1, keepdims=True) * (1.0 / WIDE) + EPS)
    centred = shifted * inverse
    scaled = (gn0[...] + gn1[...].astype(F32)) * (1.0 + modr[1:2, :])
    first = jnp.sum(scaled, axis=1, keepdims=True) * (1.0 / WIDE)
    second = jnp.sum(scaled * centred, axis=1, keepdims=True) * (1.0 / WIDE)
    gm_o[...] = (c0[...].astype(F32) + inverse * (scaled - first - centred * second)).astype(BF16)
    mixed_o[...] = (stream + modr[2:3, :] * (op0[...] + op1[...].astype(F32))).astype(BF16)


def spatial_backward(
    me_ref, g0, g1, g2, g3, x0, x1, x2, x3, q_r, k_r, v_r, st, modr, modc, gains, wo, wn,
    p0, p1, p2, p3, rs_o, gown, da_s, gq_s,
):
    me = me_ref[0]
    gk = [None] * PER
    gv = [None] * PER
    for d, g in enumerate((g0, g1, g2, g3)):
        columns = pl.ds(pl.multiple_of((me ^ d) * OWN, OWN), OWN)
        gated = (modr[2:3, :] * g[...].astype(F32)).astype(BF16)
        grad_att = dot(wo[...], gated, (1, 1)).astype(BF16)
        queries = q_r[:, columns]
        for h in range(PER):
            rows = slice(h * HEAD, (h + 1) * HEAD)
            q, k, v, da = queries[rows], k_r[rows, :], v_r[rows, :], grad_att[rows]
            scores = dot(k, q, (0, 0))
            unnormed = jnp.exp2(scores * (SCALE * LOG2E))
            probs = unnormed * (1.0 / jnp.sum(unnormed, axis=0, keepdims=True))
            rounded = probs.astype(BF16)
            grad_probs = dot(v, da, (0, 0))
            inner = jnp.sum(grad_probs * probs, axis=0, keepdims=True)
            grad_scores = (probs * (grad_probs - inner)).astype(BF16)
            gv_t = dot(da, rounded, (1, 1))
            gk_t = dot(q, grad_scores, (1, 1))
            gv[h] = gv_t if gv[h] is None else gv[h] + gv_t
            gk[h] = gk_t if gk[h] is None else gk[h] + gk_t
            gq_s[rows, columns] = dot(k, grad_scores, (1, 0)) * SCALE
    inv_q = st[0:4, :].reshape(PER, 1, ROWS)
    inv_k = st[4:8, :].reshape(PER, 1, ROWS)
    gk = (jnp.concatenate(gk, axis=0) * SCALE).astype(BF16)
    gv = jnp.concatenate(gv, axis=0).astype(BF16)
    dq = head_back_t(gq_s[...].astype(BF16), q_r[...], inv_q, gains[:, 0:1])
    dk = head_back_t(gk, k_r[...], inv_k, gains[:, 1:2])
    stacked = jnp.concatenate([dq, dk, gv], axis=0)
    first = jnp.zeros((1, ROWS), F32)
    second = jnp.zeros((1, ROWS), F32)
    for d, x, partial in ((3, x3, p3), (1, x1, p1), (2, x2, p2), (0, x0, p0)):
        block = pl.ds(pl.multiple_of((me ^ d) * PART, 32), PART)
        term = dot(wn[block, :], stacked, (1, 0))
        partial[...] = term.astype(BF16)
        scaled = term * (1.0 + modc[block, 1:2])
        centred = (x[...].astype(F32) - st[8:9, :]) * st[9:10, :]
        first += jnp.sum(scaled, axis=0, keepdims=True)
        second += jnp.sum(scaled * centred, axis=0, keepdims=True)
    rs_o[...] = jnp.zeros_like(rs_o)
    rs_o[0:1, :] = first
    rs_o[1:2, :] = second
    for d, g in enumerate((g0, g1, g2, g3)):
        columns = pl.ds(pl.multiple_of((me ^ d) * OWN, OWN), OWN)
        da_s[...] = g[...].astype(F32).T
        gown[:, columns] = da_s[pl.ds(pl.multiple_of(me * PART, 32), PART), :].astype(BF16)


def spatial_finish(me_ref, p0, m1, o2, rs, st, x0, gown, modc, out_o):
    block = pl.ds(pl.multiple_of(me_ref[0] * PART, 32), PART)
    grad = p0[...].astype(F32) + m1[...].astype(F32) + o2[...].astype(F32)
    inverse = st[9:10, :]
    scaled = grad * (1.0 + modc[block, 1:2])
    centred = (x0[...].astype(F32) - st[8:9, :]) * inverse
    first = rs[0:1, :] * (1.0 / WIDE)
    second = rs[1:2, :] * (1.0 / WIDE)
    out_o[...] = (gown[...].astype(F32) + inverse * (scaled - first - centred * second)).astype(BF16)


def gather_rows(me_ref, c0, c1, c2, c3, rows_o, cs):
    me = me_ref[0]
    for d, c in enumerate((c0, c1, c2, c3)):
        cs[pl.ds(pl.multiple_of((me ^ d) * PART, 32), PART), :] = c[...].astype(F32)
    rows_o[...] = cs[...].T.astype(BF16)


def split_rows(me_ref, rows, c0, c1, c2, c3, cs):
    me = me_ref[0]
    cs[...] = rows[...].astype(F32).T
    for d, c in enumerate((c0, c1, c2, c3)):
        c[...] = cs[pl.ds(pl.multiple_of((me ^ d) * PART, 32), PART), :].astype(BF16)


def place_columns(me_ref, c0, c1, c2, c3, out_o):
    me = me_ref[0]
    for d, c in enumerate((c0, c1, c2, c3)):
        out_o[:, pl.ds(pl.multiple_of((me ^ d) * OWN, OWN), OWN)] = c[...]


def swap(values, d):
    return lax.ppermute(values, "head", [(i, i ^ d) for i in range(4)])


def across_seq(rows):
    moved = lax.all_to_all(
        rows.reshape(64, 2, WIDE), "seq", split_axis=0, concat_axis=0, tiled=True
    )
    return moved.reshape(OWN, WIDE)


def on_device(tokens, cotangent, qkv_weight, out_weight, modulation, head_gains):
    me = lax.axis_index("head")
    mine = me.astype(jnp.int32).reshape(1)
    wt = jnp.transpose(qkv_weight, (0, 2, 3, 1))
    modc = jnp.pad(modulation.transpose(2, 0, 1).reshape(WIDE, 6), ((0, 0), (0, 2)))
    gains = jnp.tile(head_gains.reshape(4, HEAD).T, (PER, 1))
    gains = jnp.pad(gains, ((0, 0), (0, 4)), constant_values=1.0)
    modc_s, gains_s, gains_t = modc, gains[:, 0:2], gains[:, 2:4]

    x0 = tokens.T
    x2 = swap(x0, 2)
    x1 = swap(x0, 1)
    x3 = swap(x2, 1)

    wt_t, wo_t = wt[1], out_weight[1]
    wt_far, wo_far = swap(wt_t, 2), swap(wo_t, 2)

    cot = cotangent.T
    parts = [
        lax.dynamic_slice_in_dim(cot, (me ^ d) * OWN, OWN, axis=1) for d in range(4)
    ]
    parts = [parts[0]] + [swap(parts[d], d) for d in (1, 2, 3)]
    (cot_rows,) = call(
        gather_rows, [out((OWN, WIDE))], [mine, *parts],
        [pltpu.VMEM((WIDE, OWN), F32)], smem=1,
    )
    cot0 = across_seq(cot_rows)
    cot1 = swap(cot0, 1)

    query, key, value, stats, p0, p1, p2, p3, xrow = call(
        spatial_forward,
        [out((PART, ROWS))] * 3 + [out((16, ROWS), F32)] + [out((OWN, WIDE))] * 5,
        [mine, x0, x1, x2, x3, modc_s, gains_s, wt[0], out_weight[0]],
        [pltpu.VMEM((WIDE, ROWS), BF16)],
        flops=2 * 10**9, smem=1,
    )
    m1, m3 = swap(p1, 1), swap(p3, 1)
    far = swap((p2.astype(F32) + m3.astype(F32)).astype(BF16), 2)
    branch = p0.astype(F32) + m1.astype(F32) + far.astype(F32)
    middle = (xrow.astype(F32) + modulation[0, 2][None] * branch).astype(BF16)

    t0 = across_seq(middle)
    t1 = swap(t0, 1)
    gn0, gn1, op0, op1 = call(
        temporal,
        [out((OWN, WIDE), F32), out((OWN, WIDE)), out((OWN, WIDE), F32), out((OWN, WIDE))],
        [t0, t1, cot0, cot1, modulation[1], gains_t, wt_t, wo_t, wt_far, wo_far],
        flops=3 * 10**9,
    )
    gn1, op1 = swap(gn1, 1), swap(op1, 1)
    grad_middle, mixed_rows = call(
        temporal_finish, [out((OWN, WIDE))] * 2, [t0, cot0, gn0, gn1, op0, op1, modulation[1]]
    )

    g0 = across_seq(grad_middle)
    g2 = swap(g0, 2)
    g1 = swap(g0, 1)
    g3 = swap(g2, 1)

    mixed_rows = across_seq(mixed_rows)
    parts = call(
        split_rows, [out((PART, OWN))] * 4, [mine, mixed_rows],
        [pltpu.VMEM((WIDE, OWN), F32)], smem=1,
    )
    parts = [parts[0]] + [swap(parts[d], d) for d in (1, 2, 3)]
    (mixed,) = call(place_columns, [out((PART, ROWS))], [mine, *parts], smem=1)

    wn = jnp.transpose(qkv_weight[0].reshape(WIDE, 3 * PART), (0, 1))
    p0, p1, p2, p3, sums, gown = call(
        spatial_backward,
        [out((PART, ROWS))] * 4 + [out((8, ROWS), F32), out((PART, ROWS))],
        [mine, g0, g1, g2, g3, x0, x1, x2, x3, query, key, value, stats, modulation[0], modc_s,
         gains_s, out_weight[0], wn],
        [pltpu.VMEM((WIDE, OWN), F32), pltpu.VMEM((PART, ROWS), F32)],
        flops=3 * 10**9, smem=1,
    )
    m1, m3 = swap(p1, 1), swap(p3, 1)
    sums = sums + swap(sums, 1)
    far = swap((p2.astype(F32) + m3.astype(F32)).astype(BF16), 2)
    sums = sums + swap(sums, 2)
    (grad,) = call(
        spatial_finish, [out((PART, ROWS))],
        [mine, p0, m1, far, sums, stats, x0, gown, modc_s], smem=1,
    )
    return (mixed.T, grad.T)


def solution(mesh):
    in_specs = (
        P("seq", "head"),
        P("seq", "head"),
        P(None, None, None, "head"),
        P(None, "head", None),
        P(),
        P(),
    )
    out_specs = (P("seq", "head"), P("seq", "head"))
    return jax.shard_map(
        on_device, mesh=mesh, in_specs=in_specs, out_specs=out_specs, check_vma=False
    )
```

time: 486 us -> 266 us (0.55)
  waiting for transfers between devices: 249 us -> 82.9 us
  Pallas kernels: 0 us -> 48.2 us
  matrix products: 39.2 us -> 0 us
  other arithmetic: 30.6 us -> 4.04 us
  local copies, waits for them, and re-layouts: 47.4 us -> 24.6 us
  blocking collectives: 38.4 us -> 22.3 us
  starting transfers between devices: 63.9 us -> 77.8 us
  between operations: 14.9 us -> 1.13 us
    reduce_scatter x4 -> x0, waiting for transfers between devices: 112 us -> none  [the longest x2 66.8 us: finish(): lax.psum_scatter(terms.astype(jnp.bfloat16), 'head', scatter_dimension=1,...]
    all_gather x4 -> x0, waiting for transfers between devices: 88.5 us -> none  [the longest x2 48.2 us: back_start(): gathered = lax.all_gather(grad_branch, 'head', axis=1, tiled=True)]
    ppermute x0 -> x26, waiting for transfers between devices: none -> 58.2 us  [swap(): return lax.ppermute(values, 'head', [(i, i ^ d) for i in range(4)])]
    ppermute x0 -> x26, starting transfers between devices: none -> 53.5 us  [swap(): return lax.ppermute(values, 'head', [(i, i ^ d) for i in range(4)])]
    pallas_call x0 -> x8, Pallas kernels: none -> 48.2 us  [call(): pl.pallas_call(body, out_shape=list(outs), in_specs=specs, out_specs=[pl....]
    dot_general x20 -> x0, matrix products: 39.2 us -> none  [the longest x2 5.96 us: prepare(): jnp.dot(normed, weights_in.reshape(weights_in.shape[0], 3 * local_width),...]
    all_to_all x7 -> x3, starting transfers between devices: 63.1 us -> 24.3 us  [across_seq(): lax.all_to_all(rows.reshape(64, 2, WIDE), 'seq', split_axis=0, concat_axi...]
    convert_element_type x14 -> x0, local copies, waits for them, and re-layouts: 25.8 us -> none  [the longest x6 13.7 us: head_back(): grad_f = incoming.astype(jnp.float32)]
  transfers between devices with their start and end apart: 15 -> 29, of which waited for: 12 -> 11; matrix products, arithmetic and copies ran while one was open for 15% -> 9% of each run, Pallas kernels for 0% -> 2%
where the time goes in v1:
time: 266 us; the launch traced here: 261 us
  waiting for transfers between devices  82.9 us (31%)
  starting transfers between devices  77.8 us (29%)
  Pallas kernels  48.2 us (18%)
  local copies, waits for them, and re-layouts  24.6 us (9%)
  blocking collectives  22.3 us (8%)
  other arithmetic  4.04 us (2%)
    ppermute x26, waiting for transfers between devices, swap(): return lax.ppermute(values, 'head', [(i, i ^ d) for i in range(4)])  58.2 us
    ppermute x26, starting transfers between devices, swap(): return lax.ppermute(values, 'head', [(i, i ^ d) for i in range(4)])  53.5 us
    pallas_call x8, Pallas kernels, call(): pl.pallas_call(body, out_shape=list(outs), in_specs=specs, out_specs=[pl....  48.2 us
    all_to_all x3, waiting for transfers between devices, across_seq(): lax.all_to_all(rows.reshape(64, 2, WIDE), 'seq', split_axis=0, concat_axi...  24.7 us
    all_to_all x3, starting transfers between devices, across_seq(): lax.all_to_all(rows.reshape(64, 2, WIDE), 'seq', split_axis=0, concat_axi...  24.3 us
    all_to_all x1, blocking collectives, across_seq(): lax.all_to_all(rows.reshape(64, 2, WIDE), 'seq', split_axis=0, concat_axi...  22.3 us
    unnamed x54, local copies, waits for them, and re-layouts  5.59 us
  transfers between devices with their start and end apart: 29, of which 11 were waited for; matrix products, arithmetic and copies ran while one was open for 9% of the time, Pallas kernels for 2%

profile of v1, /device:TPU:1, one launch (start us, length us, event | category | flops | bytes accessed | tf_op | source)
XLA Modules:
  0.0 260.8 jit_solution(756648727157924124)
XLA Ops:
  0.6 3.8 %collective-permute-start.1 = (bf16[288,512]{1,0:T(8,128)(2,1)}, bf16[288,512]{1,0:T(8,128)(2,1)}, u32[]{:S(2)}, u32[]{:S(2)}) collective-permute-start(bf16[288,512]{1,0:T(8,128)(2,1)} %bitcast.39), channel_id=1, source_target_pairs={{0,2},{1,3},{2,0},{3,1},{4,6},{5,7},{6,4},{7,5},{8,10},{9,11},{10,... | collective-permute-start | bytes 884744 | tf_op jit(solution)/shard_map/ppermute | solution.py:253
  5.4 3.9 %slice_bitcast_fusion = (bf16[3,288,1152]{2,1,0:T(8,128)(2,1)S(1)}, bf16[3,288,1152]{2,1,0:T(8,128)(2,1)}) fusion(bf16[2,3,288,1152]{3,2,1,0:T(8,128)(2,1)} %bitcast.35), kind=kLoop, calls=%fused_computation | loop fusion | bytes 7962624 | tf_op jit(solution)/shard_map/squeeze | solution.py:277
  9.3 1.1 collective-permute-done.1.x2
  10.5 2.3 collective-permute-start.2
  15.8 10.1 %shard_map.77 = (bf16[288,512]{1,0:T(8,128)(2,1)}, bf16[288,512]{1,0:T(8,128)(2,1)}, bf16[288,512]{1,0:T(8,128)(2,1)}, f32[16,512]{1,0:T(8,128)}, bf16[128,1152]...) custom-call(s32[1]{0:T(128)} %bitcast.me_ref, ...), custom_call_target="tpu_custom_call" | custom-call | flops 2000000000 | bytes 6265092 | tf_op jit(solution)/shard_map/pallas_call | solution.py:32
  25.8 3.0 %collective-permute-start.11 = (bf16[3,288,1152]{2,1,0:T(8,128)(2,1)S(1)}, bf16[3,288,1152]{2,1,0:T(8,128)(2,1)}, u32[]{:S(2)}, u32[]{:S(2)}) collective-permute-start(bf16[3,288,1152]{2,1,0:T(8,128)(2,1)S(1)} %get-tuple-element.52.wt_a), channel_id=1, source_target_pairs={{0,2},{1,3},{2,0},{3,1},{4,6},{5,7},{6,4},{7,5},{8,10},{9,11},{10,... | collective-permute-start | bytes 5971976 | tf_op jit(solution)/shard_map/ppermute | solution.py:253
  29.6 1.1 add_convert_fusion.2
  30.6 1.1 collective-permute-start.5
  32.8 1.8 collective-permute-start.7
  34.7 1.4 collective-permute-start.8
  36.1 43.9 %collective-permute-done.7.c2 = bf16[288,128]{1,0:T(8,128)(2,1)S(1)} collective-permute-done((bf16[288,128]{1,0:T(8,128)(2,1)S(1)}, bf16[288,128]{1,0:T(8,128)(2,1)S(1)}, u32[]{:S(2)}, u32[]{:S(2)}) %collective-permute-start.7) | collective-permute-done | bytes 73760 | tf_op jit(solution)/shard_map/ppermute | solution.py:253
  79.9 2.0 collective-permute-done.8.c3
  82.6 1.9 shard_map.78
  84.5 1.8 reshape.47
  86.4 13.0 %all-to-all-start.1 = ((bf16[64,2,1152]{2,1,0:T(2,128)(2,1)}), bf16[64,2,1152]{2,1,0:T(2,128)(2,1)S(1)}, u32[]{:S(2)}, u32[]{:S(2)}) async-start(bf16[64,2,1152]{2,1,0:T(2,128)(2,1)} %reshape.47), calls=%async_computation.1 | async-start | bytes 589824 | tf_op jit(solution)/shard_map/all_to_all | solution.py:257
  100.1 1.3 add_convert_fusion.1
  102.3 9.8 %all-to-all-done.1 = bf16[64,2,1152]{2,1,0:T(2,128)(2,1)S(1)} async-done(((bf16[64,2,1152]{2,1,0:T(2,128)(2,1)}), bf16[64,2,1152]{2,1,0:T(2,128)(2,1)S(1)}, u32[]{:S(2)}, u32[]{:S(2)}) %all-to-all-start.1) | async-done | bytes 294944 | tf_op jit(solution)/shard_map/all_to_all | solution.py:257
  112.1 5.5 %all-to-all-start = ((bf16[64,2,1152]{2,1,0:T(2,128)(2,1)}), bf16[64,2,1152]{2,1,0:T(2,128)(2,1)S(1)}, u32[]{:S(2)}, u32[]{:S(2)}) async-start(bf16[64,2,1152]{2,1,0:T(2,128)(2,1)} %reshape.45), calls=%async_computation | async-start | bytes 589824 | tf_op jit(solution)/shard_map/all_to_all | solution.py:257
  117.6 2.7 %collective-permute-start.12 = (bf16[288,1152]{1,0:T(8,128)(2,1)S(1)}, bf16[288,1152]{1,0:T(8,128)(2,1)}, u32[]{:S(2)}, u32[]{:S(2)}) collective-permute-start(bf16[288,1152]{1,0:T(8,128)(2,1)S(1)} %get-tuple-element.54.wo_a), channel_id=1, source_target_pairs={{0,2},{1,3},{2,0},{3,1},{4,6},{5,7},{6,4},{7,5},{8,10},{9,11},{10,... | collective-permute-start | bytes 1990664 | tf_op jit(solution)/shard_map/ppermute | solution.py:253
  120.4 1.7 collective-permute-start.10
  122.1 6.5 %all-to-all-done = bf16[64,2,1152]{2,1,0:T(2,128)(2,1)S(1)} async-done(((bf16[64,2,1152]{2,1,0:T(2,128)(2,1)}), bf16[64,2,1152]{2,1,0:T(2,128)(2,1)S(1)}, u32[]{:S(2)}, u32[]{:S(2)}) %all-to-all-start) | async-done | bytes 294944 | tf_op jit(solution)/shard_map/all_to_all | solution.py:257
  128.8 3.8 %collective-permute-start.9 = (bf16[128,1152]{1,0:T(8,128)(2,1)S(1)}, bf16[128,1152]{1,0:T(8,128)(2,1)S(1)}, u32[]{:S(2)}, u32[]{:S(2)}) collective-permute-start(bf16[128,1152]{1,0:T(8,128)(2,1)S(1)} %reshape.46.x0), channel_id=1, source_target_pairs={{0,1},{1,0},{2,3},{3,2},{4,5},{5,4},{6,7},{7,6},{8,9},{9,8},{10,11... | collective-permute-start | bytes 884744 | tf_op jit(solution)/shard_map/ppermute | solution.py:253
  134.0 3.7 %collective-permute-done.12.wo_b = bf16[288,1152]{1,0:T(8,128)(2,1)} collective-permute-done((bf16[288,1152]{1,0:T(8,128)(2,1)S(1)}, bf16[288,1152]{1,0:T(8,128)(2,1)}, u32[]{:S(2)}, u32[]{:S(2)}) %collective-permute-start.12) | collective-permute-done | bytes 663584 | tf_op jit(solution)/shard_map/ppermute | solution.py:253
  138.5 13.6 %shard_map.79 = (f32[128,1152]{1,0:T(8,128)}, bf16[128,1152]{1,0:T(8,128)(2,1)}, f32[128,1152]{1,0:T(8,128)}, bf16[128,1152]{1,0:T(8,128)(2,1)}) custom-call(bf16[128,1152]{1,0:T(8,128)(2,1)} %copy-done.3, bf16[128,1152]{1,0:T(8,128)(2,1)} %copy-done.25, bf16[128,1152]{1,0:T(8,128)(2,1)} %copy-done.2, bf16[128,1152]{1,0:T(8,128)(2,1)} %collective-permute-done.10.c1, ...), custom_call_target="tpu_custom_call" | custom-call | flops 3000000000 | bytes 8273664 | tf_op jit(solution)/shard_map/pallas_call | solution.py:32
  152.1 2.0 collective-permute-start.13
  154.1 8.9 %collective-permute-start.14 = (bf16[128,1152]{1,0:T(8,128)(2,1)}, bf16[128,1152]{1,0:T(8,128)(2,1)S(1)}, u32[]{:S(2)}, u32[]{:S(2)}) collective-permute-start(bf16[128,1152]{1,0:T(8,128)(2,1)} %get-tuple-element.35), channel_id=1, source_target_pairs={{0,1},{1,0},{2,3},{3,2},{4,5},{5,4},{6,7},{7,6},{8,9},{9,8},{10,11... | collective-permute-start | bytes 884744 | tf_op jit(solution)/shard_map/ppermute | solution.py:253
  163.0 1.5 collective-permute-done.14.op1
  165.2 2.8 %shard_map.80 = (bf16[128,1152]{1,0:T(8,128)(2,1)}, bf16[128,1152]{1,0:T(8,128)(2,1)}) custom-call(bf16[128,1152]{1,0:T(8,128)(2,1)} %copy-done.3, bf16[128,1152]{1,0:T(8,128)(2,1)} %copy-done.2, f32[128,1152]{1,0:T(8,128)} %get-tuple-element.32.gn0, bf16[128,1152]{1,0:T(8,128)(2,1)} %copy-done.11, f32[128,1152]{1,0:T(8,128)} %get-tuple-element.34.op0, ...), custom_call_target="tpu_custom_call" | custom-call | bytes 2962944 | tf_op jit(solution)/shard_map/pallas_call | solution.py:32
  168.0 1.1 reshape.51
  169.1 22.3 %all_to_all.20 = bf16[64,2,1152]{2,1,0:T(2,128)(2,1)S(1)} all-to-all(bf16[64,2,1152]{2,1,0:T(2,128)(2,1)S(1)} %reshape.51), channel_id=1, replica_groups=mesh['seq'=64,'head'=4] {'seq'}, dimensions={0} | all-to-all | bytes 589824 | tf_op jit(solution)/shard_map/all_to_all | solution.py:257
  191.5 2.0 collective-permute-start.19
  193.4 2.6 %collective-permute-start.18 = (bf16[128,1152]{1,0:T(8,128)(2,1)S(1)}, bf16[128,1152]{1,0:T(8,128)(2,1)S(1)}, u32[]{:S(2)}, u32[]{:S(2)}) collective-permute-start(bf16[128,1152]{1,0:T(8,128)(2,1)S(1)} %reshape.52.g0), channel_id=1, source_target_pairs={{0,1},{1,0},{2,3},{3,2},{4,5},{5,4},{6,7},{7,6},{8,9},{9,8},{10,11... | collective-permute-start | bytes 884744 | tf_op jit(solution)/shard_map/ppermute | solution.py:253
  196.1 3.1 %collective-permute-done.19.g2 = bf16[128,1152]{1,0:T(8,128)(2,1)S(1)} collective-permute-done((bf16[128,1152]{1,0:T(8,128)(2,1)S(1)}, bf16[128,1152]{1,0:T(8,128)(2,1)S(1)}, u32[]{:S(2)}, u32[]{:S(2)}) %collective-permute-start.19) | collective-permute-done | bytes 294944 | tf_op jit(solution)/shard_map/ppermute | solution.py:253
  199.2 3.3 %collective-permute-start.20 = (bf16[128,1152]{1,0:T(8,128)(2,1)S(1)}, bf16[128,1152]{1,0:T(8,128)(2,1)S(1)}, u32[]{:S(2)}, u32[]{:S(2)}) collective-permute-start(bf16[128,1152]{1,0:T(8,128)(2,1)S(1)} %collective-permute-done.19.g2), channel_id=1, source_target_pairs={{0,1},{1,0},{2,3},{3,2},{4,5},{5,4},{6,7},{7,6},{8,9},{9,8},{10,11... | collective-permute-start | bytes 884744 | tf_op jit(solution)/shard_map/ppermute | solution.py:253
  202.5 1.7 slice.43
  204.8 2.4 copy.18.wn
  208.1 13.7 %shard_map.83 = (bf16[288,512]{1,0:T(8,128)(2,1)}, bf16[288,512]{1,0:T(8,128)(2,1)}, bf16[288,512]{1,0:T(8,128)(2,1)}, bf16[288,512]{1,0:T(8,128)(2,1)}, f32[8,512]{1,0:T(8,128)}, /*index=5*/bf16[288,512]{1,0:T(8,128)(2,1)}) custom-call(s32[1]{0:T(128)} %bitcast.me_ref, bf16[128,1152]{1,0:T(8,128)(2,1)} %copy-done.7, bf16[128,1152]{1,0:T(8,128)(2,1)} %copy-done.23, ...), custom_call_target="tpu_custom_call" | custom-call | flops 3000000000 | bytes 7474948 | tf_op jit(solution)/shard_map/pallas_call | solution.py:32
  223.0 5.8 %all-to-all-start.2 = ((bf16[64,2,1152]{2,1,0:T(2,128)(2,1)}), bf16[64,2,1152]{2,1,0:T(2,128)(2,1)S(1)}, u32[]{:S(2)}, u32[]{:S(2)}) async-start(bf16[64,2,1152]{2,1,0:T(2,128)(2,1)} %reshape.49), calls=%async_computation.2 | async-start | bytes 589824 | tf_op jit(solution)/shard_map/all_to_all | solution.py:257
  230.6 2.0 collective-permute-start.23
  232.9 8.4 %all-to-all-done.2 = bf16[64,2,1152]{2,1,0:T(2,128)(2,1)S(1)} async-done(((bf16[64,2,1152]{2,1,0:T(2,128)(2,1)}), bf16[64,2,1152]{2,1,0:T(2,128)(2,1)S(1)}, u32[]{:S(2)}, u32[]{:S(2)}) %all-to-all-start.2) | async-done | bytes 294944 | tf_op jit(solution)/shard_map/all_to_all | solution.py:257
  242.1 1.8 shard_map.81
  243.9 2.3 collective-permute-start.15
  246.2 1.9 collective-permute-start.16
  248.2 1.2 collective-permute-start.17
  249.4 2.0 collective-permute-start.25
  251.9 2.4 collective-permute-done.17.c3
  254.8 1.8 shard_map.82
  258.0 2.6 shard_map.84
  (100 shorter events, 19.3 us)
Async XLA Ops:
  0.6 9.8 %collective-permute-start.1 = (bf16[288,512]{1,0:T(8,128)(2,1)}, bf16[288,512]{1,0:T(8,128)(2,1)}, u32[]{:S(2)}, u32[]{:S(2)}) collective-permute-start(bf16[288,512]{1,0:T(8,128)(2,1)} %bitcast.39), channel_id=1, source_target_pairs={{0,2},{1,3},{2,0},{3,1},{4,6},{5,7},{6,4},{7,5},{8,10},{9,11},{10,... | collective-permute-start | bytes 884744 | tf_op jit(solution)/shard_map/ppermute | solution.py:253
  4.5 11.3 %collective-permute-start = (bf16[288,512]{1,0:T(8,128)(2,1)}, bf16[288,512]{1,0:T(8,128)(2,1)}, u32[]{:S(2)}, u32[]{:S(2)}) collective-permute-start(bf16[288,512]{1,0:T(8,128)(2,1)} %bitcast.40), channel_id=1, source_target_pairs={{0,1},{1,0},{2,3},{3,2},{4,5},{5,4},{6,7},{7,6},{8,9},{9,8},{10,11... | collective-permute-start | bytes 884744 | tf_op jit(solution)/shard_map/ppermute | solution.py:253
  5.4 7.3 %copy-start.1 = (bf16[2,288,1152]{2,1,0:T(8,128)(2,1)S(1)}, bf16[2,288,1152]{2,1,0:T(8,128)(2,1)}, u32[]{:S(2)}) copy-start(bf16[2,288,1152]{2,1,0:T(8,128)(2,1)} %param.9) | copy-start | bytes 3981316
  9.3 16.5 %copy-start = (bf16[3,288,1152]{2,1,0:T(8,128)(2,1)}, bf16[3,288,1152]{2,1,0:T(8,128)(2,1)S(1)}, u32[]{:S(2)}) copy-start(bf16[3,288,1152]{2,1,0:T(8,128)(2,1)S(1)} %get-tuple-element.52.wt_a) | copy-start | bytes 5971972
  9.3 4.4 %copy-start.13 = (f32[2,3,1152]{2,0,1:T(2,128)S(1)}, f32[2,3,1152]{2,0,1:T(2,128)}, u32[]{:S(2)}) copy-start(f32[2,3,1152]{2,0,1:T(2,128)} %param.10) | copy-start | bytes 82948
  9.3 4.7 %copy-start.21 = (f32[2,2,72]{2,1,0:T(2,128)S(1)}, f32[2,2,72]{2,1,0:T(2,128)}, u32[]{:S(2)}) copy-start(f32[2,2,72]{2,1,0:T(2,128)} %param.11) | copy-start | bytes 3460
  10.5 5.3 %collective-permute-start.2 = (bf16[288,512]{1,0:T(8,128)(2,1)}, bf16[288,512]{1,0:T(8,128)(2,1)}, u32[]{:S(2)}, u32[]{:S(2)}) collective-permute-start(bf16[288,512]{1,0:T(8,128)(2,1)} %collective-permute-done.1.x2), channel_id=1, source_target_pairs={{0,1},{1,0},{2,3},{3,2},{4,5},{5,4},{6,7},{7,6},{8,9},{9,8},{10,11... | collective-permute-start | bytes 884744 | tf_op jit(solution)/shard_map/ppermute | solution.py:253
  13.7 103.9 %copy-start.4 = (bf16[288,1152]{1,0:T(8,128)(2,1)}, bf16[288,1152]{1,0:T(8,128)(2,1)S(1)}, u32[]{:S(2)}) copy-start(bf16[288,1152]{1,0:T(8,128)(2,1)S(1)} %get-tuple-element.54.wo_a) | copy-start | bytes 1990660
  15.8 16.0 %copy-start.5 = (bf16[512,288]{0,1:T(8,128)(2,1)S(1)}, bf16[512,288]{0,1:T(8,128)(2,1)}, u32[]{:S(2)}) copy-start(bf16[512,288]{0,1:T(8,128)(2,1)} %param.7) | copy-start | bytes 884740
  25.8 3.8 %collective-permute-start.4 = (bf16[128,1152]{1,0:T(8,128)(2,1)}, bf16[128,1152]{1,0:T(8,128)(2,1)S(1)}, u32[]{:S(2)}, u32[]{:S(2)}) collective-permute-start(bf16[128,1152]{1,0:T(8,128)(2,1)} %get-tuple-element.31), channel_id=1, source_target_pairs={{0,1},{1,0},{2,3},{3,2},{4,5},{5,4},{6,7},{7,6},{8,9},{9,8},{10,11... | collective-permute-start | bytes 884744 | tf_op jit(solution)/shard_map/ppermute | solution.py:253
  25.8 111.9 %collective-permute-start.11 = (bf16[3,288,1152]{2,1,0:T(8,128)(2,1)S(1)}, bf16[3,288,1152]{2,1,0:T(8,128)(2,1)}, u32[]{:S(2)}, u32[]{:S(2)}) collective-permute-start(bf16[3,288,1152]{2,1,0:T(8,128)(2,1)S(1)} %get-tuple-element.52.wt_a), channel_id=1, source_target_pairs={{0,2},{1,3},{2,0},{3,1},{4,6},{5,7},{6,4},{7,5},{8,10},{9,11},{10,... | collective-permute-start | bytes 5971976 | tf_op jit(solution)/shard_map/ppermute | solution.py:253
  28.9 71.2 %collective-permute-start.3 = (bf16[128,1152]{1,0:T(8,128)(2,1)}, bf16[128,1152]{1,0:T(8,128)(2,1)}, u32[]{:S(2)}, u32[]{:S(2)}) collective-permute-start(bf16[128,1152]{1,0:T(8,128)(2,1)} %get-tuple-element.29), channel_id=1, source_target_pairs={{0,1},{1,0},{2,3},{3,2},{4,5},{5,4},{6,7},{7,6},{8,9},{9,8},{10,11... | collective-permute-start | bytes 884744 | tf_op jit(solution)/shard_map/ppermute | solution.py:253
  30.6 69.4 %collective-permute-start.5 = (bf16[128,1152]{1,0:T(8,128)(2,1)S(1)}, bf16[128,1152]{1,0:T(8,128)(2,1)}, u32[]{:S(2)}, u32[]{:S(2)}) collective-permute-start(bf16[128,1152]{1,0:T(8,128)(2,1)S(1)} %add_convert_fusion.2), channel_id=1, source_target_pairs={{0,2},{1,3},{2,0},{3,1},{4,6},{5,7},{6,4},{7,5},{8,10},{9,11},{10,... | collective-permute-start | bytes 884744 | tf_op jit(solution)/shard_map/ppermute | solution.py:253
  32.4 67.7 %copy-start.8 = (bf16[128,1152]{1,0:T(8,128)(2,1)S(1)}, bf16[128,1152]{1,0:T(8,128)(2,1)}, u32[]{:S(2)}) copy-start(bf16[128,1152]{1,0:T(8,128)(2,1)} %get-tuple-element.28) | copy-start | bytes 884740
  32.4 2.3 collective-permute-start.6
  32.8 47.1 %collective-permute-start.7 = (bf16[288,128]{1,0:T(8,128)(2,1)S(1)}, bf16[288,128]{1,0:T(8,128)(2,1)S(1)}, u32[]{:S(2)}, u32[]{:S(2)}) collective-permute-start(bf16[288,128]{1,0:T(8,128)(2,1)S(1)} %get-tuple-element.59), channel_id=1, source_target_pairs={{0,2},{1,3},{2,0},{3,1},{4,6},{5,7},{6,4},{7,5},{8,10},{9,11},{10,... | collective-permute-start | bytes 221192 | tf_op jit(solution)/shard_map/ppermute | solution.py:253
  34.7 47.3 %copy-start.17 = (bf16[288,128]{1,0:T(8,128)(2,1)}, bf16[288,128]{1,0:T(8,128)(2,1)S(1)}, u32[]{:S(2)}) copy-start(bf16[288,128]{1,0:T(8,128)(2,1)S(1)} %collective-permute-done.6.c1) | copy-start | bytes 221188
  34.7 47.3 %collective-permute-start.8 = (bf16[288,128]{1,0:T(8,128)(2,1)S(1)}, bf16[288,128]{1,0:T(8,128)(2,1)S(1)}, u32[]{:S(2)}, u32[]{:S(2)}) collective-permute-start(bf16[288,128]{1,0:T(8,128)(2,1)S(1)} %get-tuple-element.56), channel_id=1, source_target_pairs={{0,3},{1,2},{2,1},{3,0},{4,7},{5,6},{6,5},{7,4},{8,11},{9,10},{10,... | collective-permute-start | bytes 221192 | tf_op jit(solution)/shard_map/ppermute | solution.py:253
  79.9 2.0 copy-start.18
  86.4 25.7 %all-to-all-start.1 = ((bf16[64,2,1152]{2,1,0:T(2,128)(2,1)}), bf16[64,2,1152]{2,1,0:T(2,128)(2,1)S(1)}, u32[]{:S(2)}, u32[]{:S(2)}) async-start(bf16[64,2,1152]{2,1,0:T(2,128)(2,1)} %reshape.47), calls=%async_computation.1 | async-start | bytes 589824 | tf_op jit(solution)/shard_map/all_to_all | solution.py:257
  112.1 16.6 %all-to-all-start = ((bf16[64,2,1152]{2,1,0:T(2,128)(2,1)}), bf16[64,2,1152]{2,1,0:T(2,128)(2,1)S(1)}, u32[]{:S(2)}, u32[]{:S(2)}) async-start(bf16[64,2,1152]{2,1,0:T(2,128)(2,1)} %reshape.45), calls=%async_computation | async-start | bytes 589824 | tf_op jit(solution)/shard_map/all_to_all | solution.py:257
  117.6 20.2 %collective-permute-start.12 = (bf16[288,1152]{1,0:T(8,128)(2,1)S(1)}, bf16[288,1152]{1,0:T(8,128)(2,1)}, u32[]{:S(2)}, u32[]{:S(2)}) collective-permute-start(bf16[288,1152]{1,0:T(8,128)(2,1)S(1)} %get-tuple-element.54.wo_a), channel_id=1, source_target_pairs={{0,2},{1,3},{2,0},{3,1},{4,6},{5,7},{6,4},{7,5},{8,10},{9,11},{10,... | collective-permute-start | bytes 1990664 | tf_op jit(solution)/shard_map/ppermute | solution.py:253
  120.4 17.4 %copy-start.2 = (bf16[128,1152]{1,0:T(8,128)(2,1)}, bf16[128,1152]{1,0:T(8,128)(2,1)S(1)}, u32[]{:S(2)}) copy-start(bf16[128,1152]{1,0:T(8,128)(2,1)S(1)} %reshape.48.c0) | copy-start | bytes 884740
  120.4 17.3 %collective-permute-start.10 = (bf16[128,1152]{1,0:T(8,128)(2,1)S(1)}, bf16[128,1152]{1,0:T(8,128)(2,1)}, u32[]{:S(2)}, u32[]{:S(2)}) collective-permute-start(bf16[128,1152]{1,0:T(8,128)(2,1)S(1)} %reshape.48.c0), channel_id=1, source_target_pairs={{0,1},{1,0},{2,3},{3,2},{4,5},{5,4},{6,7},{7,6},{8,9},{9,8},{10,11... | collective-permute-start | bytes 884744 | tf_op jit(solution)/shard_map/ppermute | solution.py:253
  128.8 9.0 %copy-start.3 = (bf16[128,1152]{1,0:T(8,128)(2,1)}, bf16[128,1152]{1,0:T(8,128)(2,1)S(1)}, u32[]{:S(2)}) copy-start(bf16[128,1152]{1,0:T(8,128)(2,1)S(1)} %reshape.46.x0) | copy-start | bytes 884740
  128.8 9.0 %collective-permute-start.9 = (bf16[128,1152]{1,0:T(8,128)(2,1)S(1)}, bf16[128,1152]{1,0:T(8,128)(2,1)S(1)}, u32[]{:S(2)}, u32[]{:S(2)}) collective-permute-start(bf16[128,1152]{1,0:T(8,128)(2,1)S(1)} %reshape.46.x0), channel_id=1, source_target_pairs={{0,1},{1,0},{2,3},{3,2},{4,5},{5,4},{6,7},{7,6},{8,9},{9,8},{10,11... | collective-permute-start | bytes 884744 | tf_op jit(solution)/shard_map/ppermute | solution.py:253
  152.1 10.9 %collective-permute-start.13 = (bf16[128,1152]{1,0:T(8,128)(2,1)}, bf16[128,1152]{1,0:T(8,128)(2,1)S(1)}, u32[]{:S(2)}, u32[]{:S(2)}) collective-permute-start(bf16[128,1152]{1,0:T(8,128)(2,1)} %get-tuple-element.33), channel_id=1, source_target_pairs={{0,1},{1,0},{2,3},{3,2},{4,5},{5,4},{6,7},{7,6},{8,9},{9,8},{10,11... | collective-permute-start | bytes 884744 | tf_op jit(solution)/shard_map/ppermute | solution.py:253
  154.1 10.4 %collective-permute-start.14 = (bf16[128,1152]{1,0:T(8,128)(2,1)}, bf16[128,1152]{1,0:T(8,128)(2,1)S(1)}, u32[]{:S(2)}, u32[]{:S(2)}) collective-permute-start(bf16[128,1152]{1,0:T(8,128)(2,1)} %get-tuple-element.35), channel_id=1, source_target_pairs={{0,1},{1,0},{2,3},{3,2},{4,5},{5,4},{6,7},{7,6},{8,9},{9,8},{10,11... | collective-permute-start | bytes 884744 | tf_op jit(solution)/shard_map/ppermute | solution.py:253
  163.0 1.5 copy-start.11
  191.5 12.7 %copy-start.7 = (bf16[128,1152]{1,0:T(8,128)(2,1)}, bf16[128,1152]{1,0:T(8,128)(2,1)S(1)}, u32[]{:S(2)}) copy-start(bf16[128,1152]{1,0:T(8,128)(2,1)S(1)} %reshape.52.g0) | copy-start | bytes 884740
  191.5 7.7 %collective-permute-start.19 = (bf16[128,1152]{1,0:T(8,128)(2,1)S(1)}, bf16[128,1152]{1,0:T(8,128)(2,1)S(1)}, u32[]{:S(2)}, u32[]{:S(2)}) collective-permute-start(bf16[128,1152]{1,0:T(8,128)(2,1)S(1)} %reshape.52.g0), channel_id=1, source_target_pairs={{0,2},{1,3},{2,0},{3,1},{4,6},{5,7},{6,4},{7,5},{8,10},{9,11},{10,... | collective-permute-start | bytes 884744 | tf_op jit(solution)/shard_map/ppermute | solution.py:253
  193.4 13.8 %collective-permute-start.18 = (bf16[128,1152]{1,0:T(8,128)(2,1)S(1)}, bf16[128,1152]{1,0:T(8,128)(2,1)S(1)}, u32[]{:S(2)}, u32[]{:S(2)}) collective-permute-start(bf16[128,1152]{1,0:T(8,128)(2,1)S(1)} %reshape.52.g0), channel_id=1, source_target_pairs={{0,1},{1,0},{2,3},{3,2},{4,5},{5,4},{6,7},{7,6},{8,9},{9,8},{10,11... | collective-permute-start | bytes 884744 | tf_op jit(solution)/shard_map/ppermute | solution.py:253
  199.2 5.0 %copy-start.22 = (bf16[128,1152]{1,0:T(8,128)(2,1)}, bf16[128,1152]{1,0:T(8,128)(2,1)S(1)}, u32[]{:S(2)}) copy-start(bf16[128,1152]{1,0:T(8,128)(2,1)S(1)} %collective-permute-done.19.g2) | copy-start | bytes 884740
  199.2 8.1 %collective-permute-start.20 = (bf16[128,1152]{1,0:T(8,128)(2,1)S(1)}, bf16[128,1152]{1,0:T(8,128)(2,1)S(1)}, u32[]{:S(2)}, u32[]{:S(2)}) collective-permute-start(bf16[128,1152]{1,0:T(8,128)(2,1)S(1)} %collective-permute-done.19.g2), channel_id=1, source_target_pairs={{0,1},{1,0},{2,3},{3,2},{4,5},{5,4},{6,7},{7,6},{8,9},{9,8},{10,11... | collective-permute-start | bytes 884744 | tf_op jit(solution)/shard_map/ppermute | solution.py:253
  207.3 0.8 copy-start.24
  208.1 14.1 %copy-start.6 = (bf16[128,1152]{1,0:T(8,128)(2,1)S(1)}, bf16[128,1152]{1,0:T(8,128)(2,1)}, u32[]{:S(2)}) copy-start(bf16[128,1152]{1,0:T(8,128)(2,1)} %get-tuple-element.36) | copy-start | bytes 884740
  221.8 10.8 %copy-start.20 = (f32[8,512]{1,0:T(8,128)S(1)}, f32[8,512]{1,0:T(8,128)}, u32[]{:S(2)}) copy-start(f32[8,512]{1,0:T(8,128)} %get-tuple-element.50) | copy-start | bytes 49156
  221.8 7.8 %collective-permute-start.22 = (bf16[288,512]{1,0:T(8,128)(2,1)}, bf16[288,512]{1,0:T(8,128)(2,1)S(1)}, u32[]{:S(2)}, u32[]{:S(2)}) collective-permute-start(bf16[288,512]{1,0:T(8,128)(2,1)} %get-tuple-element.49), channel_id=1, source_target_pairs={{0,1},{1,0},{2,3},{3,2},{4,5},{5,4},{6,7},{7,6},{8,9},{9,8},{10,11... | collective-permute-start | bytes 884744 | tf_op jit(solution)/shard_map/ppermute | solution.py:253
  223.0 18.3 %all-to-all-start.2 = ((bf16[64,2,1152]{2,1,0:T(2,128)(2,1)}), bf16[64,2,1152]{2,1,0:T(2,128)(2,1)S(1)}, u32[]{:S(2)}, u32[]{:S(2)}) async-start(bf16[64,2,1152]{2,1,0:T(2,128)(2,1)} %reshape.49), calls=%async_computation.2 | async-start | bytes 589824 | tf_op jit(solution)/shard_map/all_to_all | solution.py:257
  228.8 28.4 %collective-permute-start.21 = (bf16[288,512]{1,0:T(8,128)(2,1)}, bf16[288,512]{1,0:T(8,128)(2,1)S(1)}, u32[]{:S(2)}, u32[]{:S(2)}) collective-permute-start(bf16[288,512]{1,0:T(8,128)(2,1)} %get-tuple-element.47), channel_id=1, source_target_pairs={{0,1},{1,0},{2,3},{3,2},{4,5},{5,4},{6,7},{7,6},{8,9},{9,8},{10,11... | collective-permute-start | bytes 884744 | tf_op jit(solution)/shard_map/ppermute | solution.py:253
  230.6 26.6 %collective-permute-start.23 = (bf16[288,512]{1,0:T(8,128)(2,1)S(1)}, bf16[288,512]{1,0:T(8,128)(2,1)S(1)}, u32[]{:S(2)}, u32[]{:S(2)}) collective-permute-start(bf16[288,512]{1,0:T(8,128)(2,1)S(1)} %add_convert_fusion), channel_id=1, source_target_pairs={{0,2},{1,3},{2,0},{3,1},{4,6},{5,7},{6,4},{7,5},{8,10},{9,11},{10,... | collective-permute-start | bytes 884744 | tf_op jit(solution)/shard_map/ppermute | solution.py:253
  232.6 15.6 %collective-permute-start.24 = (f32[8,512]{1,0:T(8,128)S(1)}, f32[8,512]{1,0:T(8,128)S(1)}, u32[]{:S(2)}, u32[]{:S(2)}) collective-permute-start(f32[8,512]{1,0:T(8,128)S(1)} %copy-done.20), channel_id=1, source_target_pairs={{0,1},{1,0},{2,3},{3,2},{4,5},{5,4},{6,7},{7,6},{8,9},{9,8},{10,11... | collective-permute-start | bytes 49160 | tf_op jit(solution)/shard_map/ppermute | solution.py:253
  243.9 5.5 %collective-permute-start.15 = (bf16[288,128]{1,0:T(8,128)(2,1)}, bf16[288,128]{1,0:T(8,128)(2,1)S(1)}, u32[]{:S(2)}, u32[]{:S(2)}) collective-permute-start(bf16[288,128]{1,0:T(8,128)(2,1)} %get-tuple-element.38), channel_id=1, source_target_pairs={{0,1},{1,0},{2,3},{3,2},{4,5},{5,4},{6,7},{7,6},{8,9},{9,8},{10,11... | collective-permute-start | bytes 221192 | tf_op jit(solution)/shard_map/ppermute | solution.py:253
  246.2 5.6 %collective-permute-start.16 = (bf16[288,128]{1,0:T(8,128)(2,1)}, bf16[288,128]{1,0:T(8,128)(2,1)S(1)}, u32[]{:S(2)}, u32[]{:S(2)}) collective-permute-start(bf16[288,128]{1,0:T(8,128)(2,1)} %get-tuple-element.39), channel_id=1, source_target_pairs={{0,2},{1,3},{2,0},{3,1},{4,6},{5,7},{6,4},{7,5},{8,10},{9,11},{10,... | collective-permute-start | bytes 221192 | tf_op jit(solution)/shard_map/ppermute | solution.py:253
  248.2 6.1 %collective-permute-start.17 = (bf16[288,128]{1,0:T(8,128)(2,1)}, bf16[288,128]{1,0:T(8,128)(2,1)S(1)}, u32[]{:S(2)}, u32[]{:S(2)}) collective-permute-start(bf16[288,128]{1,0:T(8,128)(2,1)} %get-tuple-element.40), channel_id=1, source_target_pairs={{0,3},{1,2},{2,1},{3,0},{4,7},{5,6},{6,5},{7,4},{8,11},{9,10},{10,... | collective-permute-start | bytes 221192 | tf_op jit(solution)/shard_map/ppermute | solution.py:253
  249.4 4.8 %copy-start.14 = (bf16[288,128]{1,0:T(8,128)(2,1)}, bf16[288,128]{1,0:T(8,128)(2,1)S(1)}, u32[]{:S(2)}) copy-start(bf16[288,128]{1,0:T(8,128)(2,1)S(1)} %collective-permute-done.15.c1) | copy-start | bytes 221188
  249.4 7.2 %collective-permute-start.25 = (f32[8,512]{1,0:T(8,128)S(1)}, f32[8,512]{1,0:T(8,128)S(1)}, u32[]{:S(2)}, u32[]{:S(2)}) collective-permute-start(f32[8,512]{1,0:T(8,128)S(1)} %add.44), channel_id=1, source_target_pairs={{0,2},{1,3},{2,0},{3,1},{4,6},{5,7},{6,4},{7,5},{8,10},{9,11},{10,... | collective-permute-start | bytes 49160 | tf_op jit(solution)/shard_map/ppermute | solution.py:253
  251.9 2.4 copy-start.15
  (7 other events, 5.0 us)
